TPU v7x, 256 devices: a whole 4x4x8 slice. The times are simulated.
256 devices in a mesh: rows: 128 (over x_lo, y, z, core), cols: 2 (over x_hi).
Axes of the slice: x: 4 (x_hi: 2, x_lo: 2; x = x_hi * 2 + x_lo), y: 4, z: 8, core: 2. Of those that a mesh axis runs over, the one named last changes fastest.
Arguments:
- features: bfloat16 [32768, 128], P('rows', 'cols'), may hold values from -6 to 6
- adj_tiles: bfloat16 [12288, 128, 128], P('rows'), may hold values from -0.109375 to 0.109375
- tile_src: int32 [12288], P('rows'), may hold values from 0 to 255, as said below
- tile_dst: int32 [12288], P('rows'), may hold values from 0 to 1, as said below
- tile_count: int32 [128], P('rows'), may hold values from 24 to 96, as said below
- cluster_size: int32 [256], P('rows'), may hold values from 64 to 128, as said below
- weight: bfloat16 [128, 256], P(None, 'cols'), may hold values from -0.5 to 0.5
- bias: float32 [256], P('cols'), may hold values from -3 to 3
- grad_out: bfloat16 [32768, 256], P('rows', 'cols'), may hold values from -6 to 6
Outputs:
- hidden: bfloat16 [32768, 256], P('rows', 'cols')
- grad_weight: float32 [128, 256], P(None, 'cols')
- grad_bias: float32 [256], P('cols')
- grad_features: bfloat16 [32768, 128], P('rows', 'cols')
Inputs may be any that keep to these rules, and one draw needn't show every extreme that they name: In row group r, slots 0 to tile_count[r] - 1 of its 96 slots hold tiles, in non-decreasing order of tile_src; the later slots are unused: their tile_src and tile_dst hold 0, and their adj_tiles hold arbitrary values that must not contribute. A used slot's column cluster belongs to row group r itself or to a row group whose index differs from r in exactly one bit (row group g holds clusters g * 2 to g * 2 + 1). Equal (row, column) pairs may repeat and then add. `tile_dst`: unused slots hold 0. `tile_count`: some row groups use all 96 slots. `cluster_size`: the real nodes of a cluster are its first ones; some cluster is full.
All inputs are finite; a program needn't handle non-finite values.
Results may differ from a plain program's by a relative error of at most 0.006.
Values may be sent and summed in bfloat16 or wider, within the bound.
A program may use at most 64 MiB of HBM per device.

v0:
```python
import math
import jax
import jax.numpy as jnp
from jax import lax
from jax.sharding import PartitionSpec as P

TILE_GROUP = 16


def sweep_slots(first_slot, last_slot, work, totals):
    turn_count = (last_slot - first_slot + TILE_GROUP - 1) // TILE_GROUP

    def one_turn(turn_index, carried):
        slot_ids = first_slot + turn_index * TILE_GROUP + jnp.arange(TILE_GROUP, dtype=jnp.int32)
        return work(carried, slot_ids, slot_ids < last_slot)

    return lax.fori_loop(0, jnp.maximum(turn_count, 0), one_turn, totals)


def slot_bounds(sources, first_slot, last_slot, low_cluster, high_cluster):
    positions = jnp.arange(sources.shape[0], dtype=jnp.int32)
    inside = (positions >= first_slot) & (positions < last_slot)
    below_low = jnp.sum((inside & (sources < low_cluster)).astype(jnp.int32))
    below_high = jnp.sum((inside & (sources < high_cluster)).astype(jnp.int32))
    return (first_slot + below_low, first_slot + below_high)


def gather_products(
    totals, tile_data, sources, targets, slot_ids, is_valid, row_table, base_cluster
):
    clamped = jnp.minimum(slot_ids, tile_data.shape[0] - 1)
    tile_block = tile_data[clamped]
    from_rows = jnp.clip(sources[clamped] - base_cluster, 0, row_table.shape[0] - 1)
    products = jnp.einsum(
        "tij,tjf->tif", tile_block, row_table[from_rows], preferred_element_type=jnp.float32
    )
    placed = jnp.where(is_valid, targets[clamped], totals.shape[0])
    return totals.at[placed].add(products, mode="drop")


def spread_products(totals, tile_data, sources, targets, slot_ids, is_valid, grad_table):
    clamped = jnp.minimum(slot_ids, tile_data.shape[0] - 1)
    tile_block = tile_data[clamped]
    products = jnp.einsum(
        "tji,tjf->tif", tile_block, grad_table[targets[clamped]], preferred_element_type=jnp.float32
    )
    placed = jnp.where(is_valid, sources[clamped], totals.shape[0])
    return totals.at[placed].add(products, mode="drop")


def local(
    features, adj_tiles, tile_src, tile_dst, tile_count, cluster_size, weight, bias, grad_out
):
    clusters_here = cluster_size.shape[0]
    tile_width = adj_tiles.shape[1]
    feat_half = features.shape[1]
    node_rows = clusters_here * tile_width
    node_ids = jnp.arange(tile_width, dtype=jnp.int32)
    live_node = (node_ids[None, :] < cluster_size[:, None]).astype(jnp.float32)[:, :, None]
    live_flat = live_node.reshape(node_rows, 1)
    masked = (
        features.reshape(clusters_here, tile_width, feat_half).astype(jnp.float32) * live_node
    ).astype(jnp.bfloat16)
    my_count = tile_count[0]
    zero_totals = jnp.zeros((clusters_here, tile_width, feat_half), jnp.float32)
    whole_rows = lax.all_gather(masked, "rows", axis=0, tiled=True)
    row_count = whole_rows.shape[0]
    first_slot, last_slot = slot_bounds(tile_src, 0, my_count, 0, 0 + row_count)
    own_totals = sweep_slots(
        first_slot,
        last_slot,
        lambda totals, slot_ids, is_valid: gather_products(
            totals, adj_tiles, tile_src, tile_dst, slot_ids, is_valid, whole_rows, 0
        ),
        zero_totals,
    )
    agg_local = own_totals.reshape(node_rows, feat_half).astype(jnp.bfloat16)
    agg_full = lax.all_gather(agg_local, "cols", axis=1, tiled=True)
    pre_activation = jnp.dot(agg_full, weight, preferred_element_type=jnp.float32) + bias
    sigmoid_pre = jax.nn.sigmoid(pre_activation)
    hidden = (pre_activation * sigmoid_pre * live_flat).astype(jnp.bfloat16)
    grad_pre = (
        grad_out.astype(jnp.float32)
        * sigmoid_pre
        * (1.0 + pre_activation * (1.0 - sigmoid_pre))
        * live_flat
    ).astype(jnp.bfloat16)
    weight_term = lax.dot_general(
        agg_full, grad_pre, (((0,), (0,)), ((), ())), preferred_element_type=jnp.float32
    )
    bias_term = jnp.sum(grad_pre.astype(jnp.float32), axis=0)
    weight_total, bias_total = lax.psum((weight_term, bias_term), "rows")
    grad_scale = 1.0 / math.sqrt(node_rows * lax.axis_size("rows"))
    grad_weight = weight_total * grad_scale
    grad_bias = bias_total * grad_scale
    partial_value = lax.dot_general(
        grad_pre, weight, (((1,), (1,)), ((), ())), preferred_element_type=jnp.float32
    )
    grad_agg = (
        lax.psum_scatter(partial_value, "cols", scatter_dimension=1, tiled=True)
        .astype(jnp.bfloat16)
        .reshape(clusters_here, tile_width, feat_half)
    )
    start_row = jnp.int32(0)
    totals = jnp.zeros((clusters_here * lax.axis_size("rows"), tile_width, feat_half), jnp.float32)
    first_slot, last_slot = slot_bounds(
        tile_src, 0, my_count, start_row, start_row + clusters_here * lax.axis_size("rows")
    )
    summed = lax.psum_scatter(
        sweep_slots(
            first_slot,
            last_slot,
            lambda carried, slot_ids, is_valid: spread_products(
                carried, adj_tiles, tile_src, tile_dst, slot_ids, is_valid, grad_agg
            ),
            totals,
        ),
        "rows",
        scatter_dimension=0,
        tiled=True,
    )
    grad_features = (summed * live_node).reshape(node_rows, feat_half).astype(jnp.bfloat16)
    return (hidden, grad_weight, grad_bias, grad_features)


def solution(mesh):
    return jax.shard_map(
        local,
        mesh=mesh,
        in_specs=(
            P("rows", "cols"),
            P("rows", None, None),
            P("rows"),
            P("rows"),
            P("rows"),
            P("rows"),
            P(None, "cols"),
            P("cols"),
            P("rows", "cols"),
        ),
        out_specs=(P("rows", "cols"), P(None, "cols"), P("cols"), P("rows", "cols")),
        check_vma=False,
    )
```

profile of v0, /device:TPU:4, one launch (start us, length us, event | category | flops | bytes accessed | tf_op | source)
XLA Modules:
  0.0 1835.9 jit_solution(9324555501634384926)
XLA Ops:
  10.1 1.4 fusion.8
  12.8 216.2 %all-gather.2.cloned.1.call-done = bf16[256,128,64]{1,2,0:T(8,128)(2,1)} async-done(((bf16[2,128,64]{1,2,0:T(8,128)(2,1)}), bf16[256,128,64]{1,2,0:T(8,128)(2,1)}) %all-gather.2.cloned.1.call-update) | async-done | bytes 4194320 | tf_op jit(solution)/shard_map/all_gather | solution.py:66
  229.0 8.4 copy.27
  237.4 33.4 %while.20 = (s32[]{:T(128)}, f32[2,128,64]{1,2,0:T(8,128)S(1)}, s32[]{:T(128)}, s32[]{:T(128)}, s32[]{:T(128)}, /*index=5*/s32[96]{0:T(128)S(1)}, bf16[96,128,12...) while((s32[]{:T(128)}, f32[2,128,64]{1,2,0:T(8,128)S(1)}, ...), condition=%wide.region_4.5_spmd, body=%wide.region_2.4_spmd.sunk | while | flops 33687796 | bytes 4465809 | solution.py:17
  240.1 4.0 gather_fusion.3
  244.1 2.5 gather_fusion.1
  251.2 4.0 gather_fusion.3
  255.3 2.5 gather_fusion.1
  262.3 4.0 gather_fusion.3
  266.4 2.5 gather_fusion.1
  270.8 6.1 all_gather.7
  279.5 44.7 %reduce-scatter.3.cloned.1.call-done = f32[256,64]{0,1:T(8,128)} async-done(((f32[256,128]{0,1:T(8,128)}), f32[256,64]{0,1:T(8,128)}) %reduce-scatter.3.cloned.1.call-update) | async-done | bytes 65552 | tf_op jit(solution)/shard_map/reduce_scatter | solution.py:100
  325.2 4.3 broadcast_in_dim.17
  329.5 26.7 %while.21 = (s32[]{:T(128)}, f32[256,128,64]{1,2,0:T(8,128)}, s32[]{:T(128)}, s32[]{:T(128)}, s32[]{:T(128)}, /*index=5*/s32[96]{0:T(128)S(1)}, bf16[96,128,128]...) while((s32[]{:T(128)}, f32[256,128,64]{1,2,0:T(8,128)}, ...), condition=%wide.region_11.12_spmd, body=%wide.region_9.11_spmd.sunk | while | flops 33687780 | bytes 4465809 | solution.py:17
  332.8 2.5 gather_fusion.5
  335.7 2.7 scatter_fusion.1
  341.7 2.5 gather_fusion.5
  344.5 2.7 scatter_fusion.1
  350.6 2.5 gather_fusion.5
  353.5 2.7 scatter_fusion.1
  356.2 299.2 %psum.15 = f32[128]{0:T(128)S(1)} all-reduce(f32[128]{0:T(128)S(1)} %get-tuple-element.194), channel_id=1, replica_groups=mesh['rows'=128,'cols'=2] {'rows'}, use_global_device_ids=true, to_apply=%region_7.8 | all-reduce | flops 128 | bytes 1024 | tf_op jit(solution)/shard_map/psum | solution.py:92
  656.0 599.3 %all-reduce.2.cloned.1.call-done = f32[128,128]{1,0:T(8,128)} async-done(((f32[128,128]{1,0:T(8,128)}), f32[128,128]{1,0:T(8,128)}) %all-reduce.2.cloned.1.call-update) | async-done | bytes 65552 | tf_op jit(solution)/shard_map/psum | solution.py:92
  1255.2 1.5 broadcast_multiply_fusion
  1256.7 571.1 %reduce-scatter.5.cloned.1.call-done = f32[2,128,64]{1,2,0:T(8,128)} async-done(((f32[256,128,64]{1,2,0:T(8,128)}), f32[2,128,64]{1,2,0:T(8,128)}) %reduce-scatter.5.cloned.1.call-update) | async-done | bytes 65552 | tf_op jit(solution)/shard_map/reduce_scatter | solution.py:109
  (86 shorter events, 28.5 us)
Async XLA Ops:
  7.2 269.7 %copy-start = (bf16[128,128]{1,0:T(8,128)(2,1)S(1)}, bf16[128,128]{1,0:T(8,128)(2,1)}, u32[]{:S(2)}) copy-start(bf16[128,128]{1,0:T(8,128)(2,1)} %param.19) | copy-start | bytes 98308
  7.2 230.2 %copy-start.1 = (s32[96]{0:T(128)S(1)}, s32[96]{0:T(128)}, u32[]{:S(2)}) copy-start(s32[96]{0:T(128)} %param.15) | copy-start | bytes 1156
  7.2 230.2 %copy-start.2 = (s32[96]{0:T(128)S(1)}, s32[96]{0:T(128)}, u32[]{:S(2)}) copy-start(s32[96]{0:T(128)} %param.16) | copy-start | bytes 1156
  7.2 221.8 %all-gather.2.cloned.1.call-start = ((), (), s32[]{:S(2)}) async-start(), calls=%async_computation.2 | async-start | bytes 4227072 | tf_op jit(solution)/shard_map/all_gather | solution.py:66
  9.4 314.8 %reduce-scatter.3.cloned.1.call-start = ((), (), s32[]{:S(2)}) async-start(), calls=%async_computation.4 | async-start | bytes 196608 | tf_op jit(solution)/shard_map/reduce_scatter | solution.py:100
  237.4 39.5 %copy-start.3 = (bf16[256,128]{1,0:T(8,128)(2,1)S(1)}, bf16[256,128]{1,0:T(8,128)(2,1)}, u32[]{:S(2)}) copy-start(bf16[256,128]{1,0:T(8,128)(2,1)} %param.21) | copy-start | bytes 196612
  237.4 39.5 %copy-start.4 = (f32[128]{0:T(128)S(1)}, f32[128]{0:T(128)}, u32[]{:S(2)}) copy-start(f32[128]{0:T(128)} %param.20) | copy-start | bytes 1540
  278.6 976.6 %all-reduce.2.cloned.1.call-start = ((), (), s32[]{:S(2)}) async-start(), calls=%async_computation.3 | async-start | bytes 131072 | tf_op jit(solution)/shard_map/psum | solution.py:92
  279.5 1548.4 %reduce-scatter.5.cloned.1.call-start = ((), (), s32[]{:S(2)}) async-start(), calls=%async_computation.5 | async-start | bytes 8454144 | tf_op jit(solution)/shard_map/reduce_scatter | solution.py:109
Sparse Core Ops, SparseCore 0:
  10.5 218.4 all-gather.1
  278.7 45.4 reduce-scatter.2
  327.4 927.7 all-reduce.1
  1257.7 570.0 reduce-scatter.4
where the time goes:
time: 1840 us
  waiting for transfers between devices  1430 us (78%)
  blocking collectives  305 us (17%)
  local copies, waits for them, and re-layouts  52 us (3%)
  other arithmetic  22.3 us (1%)
    psum x1, waiting for transfers between devices, local(): weight_total, bias_total = lax.psum((weight_term, bias_term), 'rows')  599 us
    reduce_scatter x1, waiting for transfers between devices, local(): lax.psum_scatter(sweep_slots(first_slot, last_slot, lambda carried, slot_...  571 us
    psum x1, blocking collectives, local(): weight_total, bias_total = lax.psum((weight_term, bias_term), 'rows')  299 us
    all_gather x1, waiting for transfers between devices, local(): whole_rows = lax.all_gather(masked, 'rows', axis=0, tiled=True)  216 us
    reduce_scatter x1, waiting for transfers between devices, local(): lax.psum_scatter(partial_value, 'cols', scatter_dimension=1, tiled=True)  44.7 us
  transfers between devices with their start and end apart: 4, of which 4 were waited for; matrix products, arithmetic and copies ran while one was open for 2% of the time, Pallas kernels for 0%

commit v1 on v0

--- a/solution.py
+++ b/solution.py
@@ -63,7 +63,9 @@
     ).astype(jnp.bfloat16)
     my_count = tile_count[0]
     zero_totals = jnp.zeros((clusters_here, tile_width, feat_half), jnp.float32)
-    whole_rows = lax.all_gather(masked, "rows", axis=0, tiled=True)
+    whole_rows = jnp.concatenate(
+        lax.all_to_all(jnp.stack([masked] * lax.axis_size("rows")), "rows", 0, 0), axis=0
+    )
     row_count = whole_rows.shape[0]
     first_slot, last_slot = slot_bounds(tile_src, 0, my_count, 0, 0 + row_count)
     own_totals = sweep_slots(

time: 1840 us -> 1710 us (0.929)
  waiting for transfers between devices: 1430 us -> 1290 us
    all_gather x1 -> x0, waiting for transfers between devices: 216 us -> none  [local(): whole_rows = lax.all_gather(masked, 'rows', axis=0, tiled=True)]
    all_to_all x0 -> x1, waiting for transfers between devices: none -> 92.9 us  [local(): lax.all_to_all(jnp.stack([masked] * lax.axis_size('rows')), 'rows', 0, 0)]
where the time goes in v1:
time: 1710 us
  waiting for transfers between devices  1290 us (75%)
  blocking collectives  305 us (18%)
  local copies, waits for them, and re-layouts  54.4 us (3%)
  other arithmetic  21.7 us (1%)
  between operations  17.5 us (1%)
    psum x1, waiting for transfers between devices, local(): weight_total, bias_total = lax.psum((weight_term, bias_term), 'rows')  582 us
    reduce_scatter x1, waiting for transfers between devices, local(): lax.psum_scatter(sweep_slots(first_slot, last_slot, lambda carried, slot_...  569 us
    psum x1, blocking collectives, local(): weight_total, bias_total = lax.psum((weight_term, bias_term), 'rows')  299 us
    all_to_all x1, waiting for transfers between devices, local(): lax.all_to_all(jnp.stack([masked] * lax.axis_size('rows')), 'rows', 0, 0)  92.9 us
    reduce_scatter x1, waiting for transfers between devices, local(): lax.psum_scatter(partial_value, 'cols', scatter_dimension=1, tiled=True)  44.2 us
  transfers between devices with their start and end apart: 4, of which 4 were waited for; matrix products, arithmetic and copies ran while one was open for 2% of the time, Pallas kernels for 0%

profile of v1, /device:TPU:4, one launch (start us, length us, event | category | flops | bytes accessed | tf_op | source)
XLA Modules:
  0.0 1710.5 jit_solution(3245245534850392063)
XLA Ops:
  9.6 3.0 stack.2
  12.6 14.5 all-to-all-start
  29.8 92.9 %all-to-all-done = bf16[128,2,128,64]{2,3,1,0:T(8,128)(2,1)} async-done(((bf16[128,2,128,64]{2,3,1,0:T(8,128)(2,1)}), bf16[128,2,128,64]{2,3,1,0:T(8,128)(2,1)}, u32[]{:S(2)}, u32[]{:S(2)}) %all-to-all-start) | async-done | bytes 4194336 | tf_op jit(solution)/shard_map/all_to_all | solution.py:67
  122.8 8.4 copy.27
  131.2 33.4 %while.20 = (s32[]{:T(128)}, f32[2,128,64]{1,2,0:T(8,128)S(1)}, s32[]{:T(128)}, s32[]{:T(128)}, s32[]{:T(128)}, /*index=5*/s32[96]{0:T(128)S(1)}, bf16[96,128,12...) while((s32[]{:T(128)}, f32[2,128,64]{1,2,0:T(8,128)S(1)}, ...), condition=%wide.region_4.5_spmd, body=%wide.region_2.4_spmd.sunk | while | flops 33687796 | bytes 4465809 | solution.py:17
  133.9 4.0 gather_fusion.3
  137.9 2.5 gather_fusion.1
  145.0 4.0 gather_fusion.3
  149.0 2.5 gather_fusion.1
  156.1 4.0 gather_fusion.3
  160.1 2.5 gather_fusion.1
  164.5 6.1 all_gather.3
  173.3 44.2 %reduce-scatter.3.cloned.1.call-done = f32[256,64]{0,1:T(8,128)} async-done(((f32[256,128]{0,1:T(8,128)}), f32[256,64]{0,1:T(8,128)}) %reduce-scatter.3.cloned.1.call-update) | async-done | bytes 65552 | tf_op jit(solution)/shard_map/reduce_scatter | solution.py:102
  218.5 4.3 broadcast_in_dim.17
  222.8 26.7 %while.21 = (s32[]{:T(128)}, f32[256,128,64]{1,2,0:T(8,128)}, s32[]{:T(128)}, s32[]{:T(128)}, s32[]{:T(128)}, /*index=5*/s32[96]{0:T(128)S(1)}, bf16[96,128,128]...) while((s32[]{:T(128)}, f32[256,128,64]{1,2,0:T(8,128)}, ...), condition=%wide.region_11.12_spmd, body=%wide.region_9.11_spmd.sunk | while | flops 33687780 | bytes 4465809 | solution.py:17
  226.1 2.6 gather_fusion.5
  229.0 2.7 scatter_fusion.1
  235.0 2.6 gather_fusion.5
  237.8 2.7 scatter_fusion.1
  243.9 2.5 gather_fusion.5
  246.8 2.7 scatter_fusion.1
  249.5 299.2 %psum.15 = f32[128]{0:T(128)S(1)} all-reduce(f32[128]{0:T(128)S(1)} %get-tuple-element.176), channel_id=1, replica_groups=mesh['rows'=128,'cols'=2] {'rows'}, use_global_device_ids=true, to_apply=%region_7.8 | all-reduce | flops 128 | bytes 1024 | tf_op jit(solution)/shard_map/psum | solution.py:94
  549.2 581.8 %all-reduce.2.cloned.1.call-done = f32[128,128]{1,0:T(8,128)} async-done(((f32[128,128]{1,0:T(8,128)}), f32[128,128]{1,0:T(8,128)}) %all-reduce.2.cloned.1.call-update) | async-done | bytes 65552 | tf_op jit(solution)/shard_map/psum | solution.py:94
  1132.5 569.1 %reduce-scatter.5.cloned.1.call-done = f32[2,128,64]{1,2,0:T(8,128)} async-done(((f32[256,128,64]{1,2,0:T(8,128)}), f32[2,128,64]{1,2,0:T(8,128)}) %reduce-scatter.5.cloned.1.call-update) | async-done | bytes 65552 | tf_op jit(solution)/shard_map/reduce_scatter | solution.py:111
  (86 shorter events, 30.0 us)
Async XLA Ops:
  8.0 162.6 %copy-start = (bf16[128,128]{1,0:T(8,128)(2,1)S(1)}, bf16[128,128]{1,0:T(8,128)(2,1)}, u32[]{:S(2)}) copy-start(bf16[128,128]{1,0:T(8,128)(2,1)} %param.19) | copy-start | bytes 98308
  8.0 19.8 %copy-start.1 = (s32[96]{0:T(128)S(1)}, s32[96]{0:T(128)}, u32[]{:S(2)}) copy-start(s32[96]{0:T(128)} %param.15) | copy-start | bytes 1156
  12.6 110.2 %all-to-all-start = ((bf16[128,2,128,64]{2,3,1,0:T(8,128)(2,1)}), bf16[128,2,128,64]{2,3,1,0:T(8,128)(2,1)}, u32[]{:S(2)}, u32[]{:S(2)}) async-start(bf16[128,2,128,64]{2,3,1,0:T(8,128)(2,1)} %stack.2), calls=%async_computation | async-start | bytes 8388608 | tf_op jit(solution)/shard_map/all_to_all | solution.py:67
  27.1 104.0 %copy-start.2 = (s32[96]{0:T(128)S(1)}, s32[96]{0:T(128)}, u32[]{:S(2)}) copy-start(s32[96]{0:T(128)} %param.16) | copy-start | bytes 1156
  27.1 190.4 %reduce-scatter.3.cloned.1.call-start = ((), (), s32[]{:S(2)}) async-start(), calls=%async_computation.4 | async-start | bytes 196608 | tf_op jit(solution)/shard_map/reduce_scatter | solution.py:102
  131.1 39.5 %copy-start.3 = (bf16[256,128]{1,0:T(8,128)(2,1)S(1)}, bf16[256,128]{1,0:T(8,128)(2,1)}, u32[]{:S(2)}) copy-start(bf16[256,128]{1,0:T(8,128)(2,1)} %param.21) | copy-start | bytes 196612
  131.2 39.5 %copy-start.4 = (f32[128]{0:T(128)S(1)}, f32[128]{0:T(128)}, u32[]{:S(2)}) copy-start(f32[128]{0:T(128)} %param.20) | copy-start | bytes 1540
  172.4 958.7 %all-reduce.2.cloned.1.call-start = ((), (), s32[]{:S(2)}) async-start(), calls=%async_computation.3 | async-start | bytes 131072 | tf_op jit(solution)/shard_map/psum | solution.py:94
  173.2 1528.4 %reduce-scatter.5.cloned.1.call-start = ((), (), s32[]{:S(2)}) async-start(), calls=%async_computation.5 | async-start | bytes 8454144 | tf_op jit(solution)/shard_map/reduce_scatter | solution.py:111
Sparse Core Ops, SparseCore 0:
  172.5 44.9 reduce-scatter.2
Sparse Core Ops, SparseCore 1:
  176.0 955.0 all-reduce.1
  1133.6 567.9 reduce-scatter.4
